TPU v7x, 128 devices: a whole 4x4x4 slice. The times are simulated.
128 devices in a mesh: item: 16 (over z, y), code: 8 (over x, core).
Axes of the slice: x: 4, y: 4, z: 4, core: 2. Of those that a mesh axis runs over, the one named last changes fastest.
Arguments:
- residuals: float32 [256, 65536], P('code', 'item'), may hold values from -6 to 6
- codebook: float32 [256, 65536], P('item', 'code'), may hold values from -6 to 6
- item_weight: float32 [65536], P('item'), may hold values from 1 to 100
- code_capacity: float32 [65536], P('code'), may hold values from 0.25 to 4
- pairs: int32 [1024, 128], P('item', 'code'), may hold values from -1 to 127, as said below
Outputs:
- item_potential: float32 [65536], P('item')
- code_potential: float32 [65536], P('code')
Inputs may be any that keep to these rules, and one draw needn't show every extreme that they name: `pairs`: each entry is -1 (no candidate) or a code block's number within the code shard of its slot column. Within one item block and one code shard the live entries are distinct, the first slot is always live, and between 1 and 8 are live; some device holds exactly 8 live slots in every item block. Every code block is named by some item block.
All inputs are finite; a program needn't handle non-finite values.
Results may differ from a plain program's by a relative error of at most 0.0003.
Values sent between devices are 32-bit elements; how exact they have to be, the bound alone decides.
A program may use at most 128 MiB of HBM per device.

v0:
```python
import math
import jax
import jax.numpy as jnp
from jax import lax
from jax.sharding import PartitionSpec as P

BLOCK = 64
ITERS = 3
masked_score = -1e30
softness_factor = 0.1


def body(residuals, codebook, item_weight, code_capacity, pairs):
    item_columns = lax.all_gather(residuals, "code", axis=0, tiled=True)
    code_cols = lax.all_gather(codebook, "item", axis=0, tiled=True)
    embedding_width = item_columns.shape[0]
    item_count = item_columns.shape[1]
    code_count = code_cols.shape[1]
    item_blocks = item_count // BLOCK
    code_blocks = code_count // BLOCK
    logit_scale = 1.0 / (softness_factor * math.sqrt(embedding_width))
    weight_sum = lax.psum(jnp.sum(item_weight), "item")
    capacity_sum = lax.psum(jnp.sum(code_capacity), "code")
    item_logmass = jnp.log(item_weight) - jnp.log(weight_sum)
    code_logmass = jnp.log(code_capacity) - jnp.log(capacity_sum)
    is_live = pairs >= 0
    safe_ids = jnp.where(is_live, pairs, 0)
    target = jnp.where(is_live, pairs, code_blocks)
    item_split_cols = item_columns.reshape(embedding_width, item_blocks, BLOCK)
    code_column_splits = code_cols.reshape(embedding_width, code_blocks, BLOCK)
    group = math.gcd(item_blocks, 8)
    group_count = item_blocks // group

    def build_tiles(own, ids, live):
        picked = code_column_splits[:, ids, :]
        scores = (
            jnp.einsum("rbi,rbsj->bsij", own, picked, precision=lax.Precision.HIGHEST) * logit_scale
        )
        return jnp.where(live[:, :, None, None], scores, masked_score)

    reduce_fn = lambda tiles, ids, portion: tiles

    def one_group(group_index):
        start = group_index * group
        own = lax.dynamic_slice_in_dim(item_split_cols, start, group, 1)
        ids = lax.dynamic_slice_in_dim(safe_ids, start, group, 0)
        live = lax.dynamic_slice_in_dim(is_live, start, group, 0)
        portion = lax.dynamic_slice_in_dim(safe_ids, start, group, 0)
        return reduce_fn(build_tiles(own, ids, live), ids, portion)

    results = lax.map(one_group, jnp.arange(group_count, dtype=jnp.int32))
    saved_tile_blocks = results.reshape((item_blocks,) + results.shape[2:])

    def run_pass(reduce_fn, extra):
        return reduce_fn(saved_tile_blocks, safe_ids, extra)

    flat_target = target.reshape(-1)
    flat_rows = flat_target.shape[0]
    row_group = math.gcd(flat_rows, 256)
    one_hot = flat_target[:, None] == jnp.arange(code_blocks, dtype=jnp.int32)[None, :]
    one_hot_groups = one_hot.reshape(flat_rows // row_group, row_group, code_blocks)
    one_hot_float = one_hot.astype(jnp.float32)
    code_potential = jnp.zeros((code_count,), jnp.float32)
    item_potential = jnp.zeros((item_count,), jnp.float32)
    for sweep in range(ITERS):
        code_split = code_potential.reshape(code_blocks, BLOCK)

        def row_reduce(tiles, ids, portion):
            logits = tiles + code_split[ids][:, :, None, :]
            block_peak = jnp.max(logits, axis=(1, 3))
            block_total = jnp.sum(jnp.exp(logits - block_peak[:, None, :, None]), axis=(1, 3))
            return (block_peak, block_total)

        row_peak, row_total = run_pass(row_reduce, safe_ids)
        row_peak = row_peak.reshape(item_count)
        row_total = row_total.reshape(item_count)
        merged_peak = lax.pmax(row_peak, "code")
        merged_total = lax.psum(row_total * jnp.exp(row_peak - merged_peak), "code")
        item_potential = item_logmass - (merged_peak + jnp.log(merged_total))
        item_split = item_potential.reshape(item_blocks, BLOCK)

        def col_reduce(tiles, ids, portion):
            logits = tiles + portion[:, None, :, None]
            block_peak = jnp.max(logits, axis=2)
            block_total = jnp.sum(jnp.exp(logits - block_peak[:, :, None, :]), axis=2)
            return (block_peak, block_total)

        tile_peak, tile_total = run_pass(col_reduce, item_split)
        peak_flat = tile_peak.reshape(flat_rows, BLOCK)
        total_flat = tile_total.reshape(flat_rows, BLOCK)
        peak_groups = peak_flat.reshape(flat_rows // row_group, row_group, BLOCK)

        def peak_step(carry, pieces):
            hot, peaks = pieces
            candidate = jnp.max(jnp.where(hot[:, :, None], peaks[:, None, :], masked_score), axis=0)
            return (jnp.maximum(carry, candidate), None)

        col_peak, unused = lax.scan(
            peak_step,
            jnp.full((code_blocks, BLOCK), masked_score, jnp.float32),
            (one_hot_groups, peak_groups),
        )
        padded_peak = jnp.concatenate(
            [col_peak, jnp.full((1, BLOCK), masked_score, jnp.float32)], axis=0
        )
        spread = total_flat * jnp.exp(peak_flat - padded_peak[flat_target])
        col_total = jnp.dot(
            one_hot_float.T,
            spread,
            precision=lax.Precision.HIGHEST,
            preferred_element_type=jnp.float32,
        )
        col_peak = col_peak.reshape(code_count)
        col_total = col_total.reshape(code_count)
        joined_peak = lax.pmax(col_peak, "item")
        joined_total = lax.psum(col_total * jnp.exp(col_peak - joined_peak), "item")
        code_potential = code_logmass - (joined_peak + jnp.log(joined_total))
    return (item_potential, code_potential)


def solution(mesh):
    placed = (P("code", "item"), P("item", "code"), P("item"), P("code"), P("item", "code"))
    return jax.shard_map(
        body, mesh=mesh, in_specs=placed, out_specs=(P("item"), P("code")), check_vma=False
    )
```

profile of v0, /device:TPU:0, one launch (start us, length us, event | category | flops | bytes accessed | tf_op | source)
XLA Modules:
  0.0 1095.6 jit_solution(9727637983515556993)
XLA Ops:
  10.0 42.6 %psum.56 = f32[]{:T(128)} all-reduce(f32[]{:T(128)} %reduce_sum.72), channel_id=1, replica_groups=mesh['item'=16,'code'=8] {'item'}, use_global_device_ids=true, to_apply=%region_1.0 | all-reduce | flops 1 | bytes 8 | tf_op jit(solution)/shard_map/psum | solution.py:22
  64.6 52.7 %all-gather.3.cloned.1.call-done = f32[256,8192]{1,0:T(8,128)} async-done(((f32[16,8192]{1,0:T(8,128)}), f32[256,8192]{1,0:T(8,128)}) %all-gather.3.cloned.1.call-update) | async-done | bytes 8388624 | tf_op jit(solution)/shard_map/all_gather | solution.py:15
  126.3 158.7 %while.43 = (s32[]{:T(128)}, f32[8,8,16,64,64]{3,4,2,1,0:T(8,128)}, s32[8]{0:T(128)S(1)}, pred[64,16]{1,0:T(8,128)(4,1)S(1)}, s32[64,16]{1,0:T(8,128)S(1)}, /*in...) while((s32[]{:T(128)}, f32[8,8,16,64,64]{3,4,2,1,0:T(8,128)}, ...), condition=%wide.region_3.0_spmd, body=%wide.region_2.0_spmd.sunk | while | flops 1611662720 | bytes 29892660 | solution.py:51
  308.9 25.5 %pmax.42 = f32[4096]{0:T(1024)S(1)} all-reduce(f32[4096]{0:T(1024)S(1)} %reshape.211), channel_id=1, replica_groups=mesh['item'=16,'code'=8] {'code'}, use_global_device_ids=true, to_apply=%region_7.8 | all-reduce | flops 4096 | bytes 32768 | tf_op jit(solution)/shard_map/pmax | solution.py:77
  334.4 24.6 %all-reduce.3 = (f32[4096]{0:T(1024)S(1)}, f32[]{:T(128)}) all-reduce(f32[4096]{0:T(1024)S(1)} %exponential_multiply_fusion.5, f32[]{:T(128)} %reduce_sum.73), channel_id=1, replica_groups=mesh['item'=16,'code'=8] {'code'}, use_global_device_ids=true, to_apply=%region_9.10 | all-reduce | flops 4097 | bytes 32776 | tf_op jit(solution)/shard_map/psum | solution.py:78
  359.1 15.3 %add_reduce_fusion.4 = f32[8,8,16,64]{3,2,1,0:T(8,128)S(1)} fusion(f32[8,8,16,64,64]{3,4,2,1,0:T(8,128)} %get-tuple-element.105, f32[8,8,64]{2,1,0:T(8,128)S(1)} %add.154), kind=kLoop, calls=%fused_computation.36 | loop fusion | flops 8323072 | bytes 17055744 | tf_op jit(solution)/shard_map/reduce_max | solution.py:84
  374.4 20.7 %exponential_reduce_fusion.4 = f32[8,8,16,64]{3,2,1,0:T(8,128)S(1)} fusion(f32[8,8,16,64,64]{3,4,2,1,0:T(8,128)} %get-tuple-element.105, f32[8,8,16,64]{3,2,1,0:T(8,128)S(1)} %add_reduce_fusion.4, f32[8,8,64]{2,1,0:T(8,128)S(1)} %add.154), kind=kLoop, calls=%fused_computation.30 | loop fusion | flops 12517376 | bytes 17317888 | tf_op jit(solution)/shard_map/reduce_sum | solution.py:85
  395.1 13.3 %while.44 = (s32[]{:T(128)}, f32[128,64]{0,1:T(8,128)S(1)}, pred[4,256,128]{2,1,0:T(8,128)(4,1)S(1)}, f32[4,256,64]{2,1,0:T(8,128)S(1)}, s32[]{:T(128)}, /*index=5*/s32[]{:T(128)}) while((s32[]{:T(128)}, f32[128,64]{0,1:T(8,128)S(1)}, pred[4,256,128]{2,1,0:T(8,128)(4,1)S(1)}, f32[4,256,64]{2,1,0:T(8,128)S(1)}, s32[]{:T(128)}, ...), condition=%wide.region_13.14_spmd.clone, body=%wide.region_11.13_spmd.clone.sunk | while | flops 4202499 | bytes 426071 | solution.py:98
  412.4 72.4 %pmax.43 = f32[8192]{0:T(1024)S(1)} all-reduce(f32[8192]{0:T(1024)S(1)} %reshape.213), channel_id=1, replica_groups=mesh['item'=16,'code'=8] {'item'}, use_global_device_ids=true, to_apply=%region_14.15 | all-reduce | flops 8192 | bytes 65536 | tf_op jit(solution)/shard_map/pmax | solution.py:115
  484.8 69.5 %psum.59 = f32[8192]{0:T(1024)S(1)} all-reduce(f32[8192]{0:T(1024)S(1)} %exponential_multiply_fusion.2), channel_id=1, replica_groups=mesh['item'=16,'code'=8] {'item'}, use_global_device_ids=true, to_apply=%region_16.17 | all-reduce | flops 8192 | bytes 65536 | tf_op jit(solution)/shard_map/psum | solution.py:116
  581.9 23.5 %pmax.44 = f32[4096]{0:T(1024)S(1)} all-reduce(f32[4096]{0:T(1024)S(1)} %reshape.219), channel_id=1, replica_groups=mesh['item'=16,'code'=8] {'code'}, use_global_device_ids=true, to_apply=%region_18.19 | all-reduce | flops 4096 | bytes 32768 | tf_op jit(solution)/shard_map/pmax | solution.py:77
  605.4 23.6 %psum.60 = f32[4096]{0:T(1024)S(1)} all-reduce(f32[4096]{0:T(1024)S(1)} %exponential_multiply_fusion.4), channel_id=1, replica_groups=mesh['item'=16,'code'=8] {'code'}, use_global_device_ids=true, to_apply=%region_20.21 | all-reduce | flops 4096 | bytes 32768 | tf_op jit(solution)/shard_map/psum | solution.py:78
  629.1 15.3 %add_reduce_fusion.2 = f32[8,8,16,64]{3,2,1,0:T(8,128)S(1)} fusion(f32[8,8,16,64,64]{3,4,2,1,0:T(8,128)} %get-tuple-element.105, f32[8,8,64]{2,1,0:T(8,128)S(1)} %add.163), kind=kLoop, calls=%fused_computation.34 | loop fusion | flops 8323072 | bytes 17055744 | tf_op jit(solution)/shard_map/reduce_max | solution.py:84
  644.4 20.7 %exponential_reduce_fusion.2 = f32[8,8,16,64]{3,2,1,0:T(8,128)S(1)} fusion(f32[8,8,16,64,64]{3,4,2,1,0:T(8,128)} %get-tuple-element.105, f32[8,8,16,64]{3,2,1,0:T(8,128)S(1)} %add_reduce_fusion.2, f32[8,8,64]{2,1,0:T(8,128)S(1)} %add.163), kind=kLoop, calls=%fused_computation.28 | loop fusion | flops 12517376 | bytes 17317888 | tf_op jit(solution)/shard_map/reduce_sum | solution.py:85
  665.0 13.3 %while.45 = (s32[]{:T(128)}, f32[128,64]{0,1:T(8,128)S(1)}, pred[4,256,128]{2,1,0:T(8,128)(4,1)S(1)}, f32[4,256,64]{2,1,0:T(8,128)S(1)}, s32[]{:T(128)}, /*index=5*/s32[]{:T(128)}) while((s32[]{:T(128)}, f32[128,64]{0,1:T(8,128)S(1)}, pred[4,256,128]{2,1,0:T(8,128)(4,1)S(1)}, f32[4,256,64]{2,1,0:T(8,128)S(1)}, s32[]{:T(128)}, ...), condition=%wide.region_24.25_spmd.clone, body=%wide.region_22.24_spmd.clone.sunk | while | flops 4202499 | bytes 426071 | solution.py:98
  682.3 69.6 %pmax.45 = f32[8192]{0:T(1024)S(1)} all-reduce(f32[8192]{0:T(1024)S(1)} %reshape.221), channel_id=1, replica_groups=mesh['item'=16,'code'=8] {'item'}, use_global_device_ids=true, to_apply=%region_25.26 | all-reduce | flops 8192 | bytes 65536 | tf_op jit(solution)/shard_map/pmax | solution.py:115
  751.9 69.5 %psum.61 = f32[8192]{0:T(1024)S(1)} all-reduce(f32[8192]{0:T(1024)S(1)} %exponential_multiply_fusion.1), channel_id=1, replica_groups=mesh['item'=16,'code'=8] {'item'}, use_global_device_ids=true, to_apply=%region_27.28 | all-reduce | flops 8192 | bytes 65536 | tf_op jit(solution)/shard_map/psum | solution.py:116
  848.3 23.5 %pmax.46 = f32[4096]{0:T(1024)S(1)} all-reduce(f32[4096]{0:T(1024)S(1)} %reshape.226), channel_id=1, replica_groups=mesh['item'=16,'code'=8] {'code'}, use_global_device_ids=true, to_apply=%region_29.30 | all-reduce | flops 4096 | bytes 32768 | tf_op jit(solution)/shard_map/pmax | solution.py:77
  871.8 23.8 %psum.62 = f32[4096]{0:T(1024)S(1)} all-reduce(f32[4096]{0:T(1024)S(1)} %exponential_multiply_fusion.3), channel_id=1, replica_groups=mesh['item'=16,'code'=8] {'code'}, use_global_device_ids=true, to_apply=%region_31.32 | all-reduce | flops 4096 | bytes 32768 | tf_op jit(solution)/shard_map/psum | solution.py:78
  895.7 15.3 %add_reduce_fusion = f32[8,8,16,64]{3,2,1,0:T(8,128)S(1)} fusion(f32[8,8,16,64,64]{3,4,2,1,0:T(8,128)} %get-tuple-element.105, f32[8,8,64]{2,1,0:T(8,128)S(1)} %add.171), kind=kLoop, calls=%fused_computation.32 | loop fusion | flops 8323072 | bytes 17055744 | tf_op jit(solution)/shard_map/reduce_max | solution.py:84
  911.0 20.7 %exponential_reduce_fusion = f32[8,8,16,64]{3,2,1,0:T(8,128)S(1)} fusion(f32[8,8,16,64,64]{3,4,2,1,0:T(8,128)} %get-tuple-element.105, f32[8,8,16,64]{3,2,1,0:T(8,128)S(1)} %add_reduce_fusion, f32[8,8,64]{2,1,0:T(8,128)S(1)} %add.171), kind=kLoop, calls=%fused_computation.26 | loop fusion | flops 12517376 | bytes 17317888 | tf_op jit(solution)/shard_map/reduce_sum | solution.py:85
  931.7 13.3 %while.46 = (s32[]{:T(128)}, f32[128,64]{0,1:T(8,128)S(1)}, pred[4,256,128]{2,1,0:T(8,128)(4,1)S(1)}, f32[4,256,64]{2,1,0:T(8,128)S(1)}, s32[]{:T(128)}, /*index=5*/s32[]{:T(128)}) while((s32[]{:T(128)}, f32[128,64]{0,1:T(8,128)S(1)}, pred[4,256,128]{2,1,0:T(8,128)(4,1)S(1)}, f32[4,256,64]{2,1,0:T(8,128)S(1)}, s32[]{:T(128)}, ...), condition=%wide.region_35.36_spmd.clone, body=%wide.region_33.35_spmd.clone.sunk | while | flops 4202499 | bytes 426071 | solution.py:98
  948.9 69.6 %pmax.47 = f32[8192]{0:T(1024)S(1)} all-reduce(f32[8192]{0:T(1024)S(1)} %reshape.228), channel_id=1, replica_groups=mesh['item'=16,'code'=8] {'item'}, use_global_device_ids=true, to_apply=%region_36.37 | all-reduce | flops 8192 | bytes 65536 | tf_op jit(solution)/shard_map/pmax | solution.py:115
  1018.5 69.5 %psum.63 = f32[8192]{0:T(1024)S(1)} all-reduce(f32[8192]{0:T(1024)S(1)} %exponential_multiply_fusion), channel_id=1, replica_groups=mesh['item'=16,'code'=8] {'item'}, use_global_device_ids=true, to_apply=%region_38.39 | all-reduce | flops 8192 | bytes 65536 | tf_op jit(solution)/shard_map/psum | solution.py:116
  (193 shorter events, 306.6 us)
Async XLA Ops:
  7.2 51.8 %all-gather.5.cloned.1.call-start = ((), (), s32[]{:S(2)}) async-start(), calls=%async_computation.1 | async-start | bytes 4718592 | tf_op jit(solution)/shard_map/all_gather | solution.py:14
  7.9 109.4 %all-gather.3.cloned.1.call-start = ((), (), s32[]{:S(2)}) async-start(), calls=%async_computation | async-start | bytes 8912896 | tf_op jit(solution)/shard_map/all_gather | solution.py:15
  285.0 74.0 %copy-start.3 = (f32[4096]{0:T(1024)S(1)}, f32[4096]{0:T(1024)}, u32[]{:S(2)}) copy-start(f32[4096]{0:T(1024)} %param.15) | copy-start | bytes 49156
  359.1 195.9 %copy-start.2 = (f32[8192]{0:T(1024)S(1)}, f32[8192]{0:T(1024)}, u32[]{:S(2)}) copy-start(f32[8192]{0:T(1024)} %param.16) | copy-start | bytes 98308
  629.1 36.0 %copy-start.1 = (f32[128,64]{0,1:T(8,128)S(1)}, f32[128,64]{0,1:T(8,128)}, u32[]{:S(2)}) copy-start(f32[128,64]{0,1:T(8,128)} %custom-call.1) | copy-start | bytes 98308
  895.6 36.1 %copy-start.4 = (f32[4096]{0:T(1024)}, f32[4096]{0:T(1024)S(1)}, u32[]{:S(2)}) copy-start(f32[4096]{0:T(1024)S(1)} %add_subtract_fusion.3) | copy-start | bytes 49156
  895.7 36.0 %copy-start = (f32[128,64]{0,1:T(8,128)S(1)}, f32[128,64]{0,1:T(8,128)}, u32[]{:S(2)}) copy-start(f32[128,64]{0,1:T(8,128)} %custom-call.2) | copy-start | bytes 98308
Sparse Core Ops, SparseCore 0:
  9.7 34.5 all-gather.4
  46.4 70.8 all-gather.2
where the time goes:
time: 1100 us
  blocking collectives  607 us (55%)
  other arithmetic  222 us (20%)
  local copies, waits for them, and re-layouts  101 us (9%)
  matrix products  89.9 us (8%)
  waiting for transfers between devices  54.1 us (5%)
  between operations  15.8 us (1%)
    pmax x3, blocking collectives, body(): joined_peak = lax.pmax(col_peak, 'item')  212 us
    psum x3, blocking collectives, body(): joined_total = lax.psum(col_total * jnp.exp(col_peak - joined_peak), 'item')  209 us
    dot_general x8, matrix products, build_tiles(): jnp.einsum('rbi,rbsj->bsij', own, picked, precision=lax.Precision.HIGHEST)  87.6 us
    pmax x3, blocking collectives, body(): merged_peak = lax.pmax(row_peak, 'code')  72.6 us
    psum x3, blocking collectives, body(): merged_total = lax.psum(row_total * jnp.exp(row_peak - merged_peak), 'code')  71.9 us
    reduce_sum x3, other arithmetic, col_reduce(): block_total = jnp.sum(jnp.exp(logits - block_peak[:, :, None, :]), axis=2)  62 us
    gather x8, local copies, waits for them, and re-layouts, build_tiles(): picked = code_column_splits[:, ids, :]  61.3 us
    all_gather x1, waiting for transfers between devices, body(): code_cols = lax.all_gather(codebook, 'item', axis=0, tiled=True)  52.7 us
  transfers between devices with their start and end apart: 2, of which 1 were waited for; matrix products, arithmetic and copies ran while one was open for 1% of the time, Pallas kernels for 0%

commit v1 on v0

--- a/solution.py
+++ b/solution.py
@@ -12,7 +12,25 @@
 
 def body(residuals, codebook, item_weight, code_capacity, pairs):
     item_columns = lax.all_gather(residuals, "code", axis=0, tiled=True)
-    code_cols = lax.all_gather(codebook, "item", axis=0, tiled=True)
+    peers, index, width = (lax.axis_size("item"), lax.axis_index("item"), codebook.shape[0])
+    right = [(i, (i + 1) % peers) for i in range(peers)]
+    backward = [(i, (i - 1) % peers) for i in range(peers)]
+    code_cols = jnp.zeros(
+        (*codebook.shape[:0], peers * width, *codebook.shape[0 + 1 :]), codebook.dtype
+    )
+    code_cols = lax.dynamic_update_slice_in_dim(code_cols, codebook, index * width, axis=0)
+    from_left = from_right = codebook
+    half = peers // 2
+    for step in range(1, half + 1):
+        from_left = lax.ppermute(from_left, "item", right)
+        code_cols = lax.dynamic_update_slice_in_dim(
+            code_cols, from_left, (index - step) % peers * width, axis=0
+        )
+        if step < peers - half:
+            from_right = lax.ppermute(from_right, "item", backward)
+            code_cols = lax.dynamic_update_slice_in_dim(
+                code_cols, from_right, (index + step) % peers * width, axis=0
+            )
     embedding_width = item_columns.shape[0]
     item_count = item_columns.shape[1]
     code_count = code_cols.shape[1]

time: 1100 us -> 1570 us (1.43)
  local copies, waits for them, and re-layouts: 101 us -> 520 us
  starting transfers between devices: 0.08 us -> 37.5 us
    dynamic_update_slice x0 -> x16, local copies, waits for them, and re-layouts: none -> 375 us  [the longest x8 184 us: body(): lax.dynamic_update_slice_in_dim(code_cols, from_left, (index - step) % pe...]
    ppermute x0 -> x15, waiting for transfers between devices: none -> 63.6 us  [the longest x8 63.6 us: body(): from_left = lax.ppermute(from_left, 'item', right)]
    all_gather x1 -> x0, waiting for transfers between devices: 52.7 us -> none  [body(): code_cols = lax.all_gather(codebook, 'item', axis=0, tiled=True)]
    ppermute x0 -> x15, local copies, waits for them, and re-layouts: none -> 43.6 us  [the longest x8 22.6 us: body(): from_left = lax.ppermute(from_left, 'item', right)]
    ppermute x0 -> x15, starting transfers between devices: none -> 37.5 us  [the longest x7 35.7 us: body(): from_right = lax.ppermute(from_right, 'item', backward)]
  transfers between devices with their start and end apart: 2 -> 16, of which waited for: 1 -> 7; matrix products, arithmetic and copies ran while one was open for 1% -> 28% of each run, Pallas kernels for 0% -> 0%
where the time goes in v1:
time: 1570 us; the launch traced here: 1560 us
  blocking collectives  602 us (38%)
  local copies, waits for them, and re-layouts  520 us (33%)
  other arithmetic  224 us (14%)
  matrix products  89.9 us (6%)
  waiting for transfers between devices  64.3 us (4%)
  starting transfers between devices  37.5 us (2%)
  between operations  16.2 us (1%)
    psum x3, blocking collectives, body(): joined_total = lax.psum(col_total * jnp.exp(col_peak - joined_peak), 'item')  209 us
    pmax x3, blocking collectives, body(): joined_peak = lax.pmax(col_peak, 'item')  209 us
    dynamic_update_slice x8, local copies, waits for them, and re-layouts, body(): lax.dynamic_update_slice_in_dim(code_cols, from_left, (index - step) % pe...  184 us
    dynamic_update_slice x7, local copies, waits for them, and re-layouts, body(): lax.dynamic_update_slice_in_dim(code_cols, from_right, (index + step) % p...  170 us
    dot_general x8, matrix products, build_tiles(): jnp.einsum('rbi,rbsj->bsij', own, picked, precision=lax.Precision.HIGHEST)  87.6 us
    psum x3, blocking collectives, body(): merged_total = lax.psum(row_total * jnp.exp(row_peak - merged_peak), 'code')  72 us
    pmax x3, blocking collectives, body(): merged_peak = lax.pmax(row_peak, 'code')  70.6 us
    ppermute x8, waiting for transfers between devices, body(): from_left = lax.ppermute(from_left, 'item', right)  63.6 us
  transfers between devices with their start and end apart: 16, of which 7 were waited for; matrix products, arithmetic and copies ran while one was open for 28% of the time, Pallas kernels for 0%

profile of v1, /device:TPU:0, one launch (start us, length us, event | category | flops | bytes accessed | tf_op | source)
XLA Modules:
  0.0 1559.2 jit_solution(5130218817349166997)
XLA Ops:
  113.5 41.7 %psum.56 = f32[]{:T(128)} all-reduce(f32[]{:T(128)} %reduce_sum.72), channel_id=1, replica_groups=mesh['item'=16,'code'=8] {'item'}, use_global_device_ids=true, to_apply=%region_1.2 | all-reduce | flops 1 | bytes 8 | tf_op jit(solution)/shard_map/psum | solution.py:40
  218.9 24.3 %dynamic_update_slice.54 = f32[256,8192]{0,1:T(8,128)} dynamic-update-slice(f32[256,8192]{0,1:T(8,128)} %dynamic_update_slice.53, f32[16,8192]{0,1:T(8,128)} %copy.49, s32[]{:T(128)S(6)} %select_n.165, s32[]{:T(128)} %constant.156.clone.1) | dynamic-update-slice | bytes 1048580 | tf_op jit(solution)/shard_map/dynamic_update_slice | solution.py:31
  245.8 23.4 %dynamic_update_slice.55 = f32[256,8192]{0,1:T(8,128)} dynamic-update-slice(f32[256,8192]{0,1:T(8,128)} %dynamic_update_slice.54, f32[16,8192]{0,1:T(8,128)} %copy.50, s32[]{:T(128)S(6)} %select_n.167, s32[]{:T(128)} %constant.156.clone.1) | dynamic-update-slice | bytes 1048580 | tf_op jit(solution)/shard_map/dynamic_update_slice | solution.py:26
  271.9 24.3 %dynamic_update_slice.56 = f32[256,8192]{0,1:T(8,128)} dynamic-update-slice(f32[256,8192]{0,1:T(8,128)} %dynamic_update_slice.55, f32[16,8192]{0,1:T(8,128)} %copy.51, s32[]{:T(128)S(6)} %select_n.169, s32[]{:T(128)} %constant.156.clone.1) | dynamic-update-slice | bytes 1048580 | tf_op jit(solution)/shard_map/dynamic_update_slice | solution.py:31
  298.8 23.4 %dynamic_update_slice.57 = f32[256,8192]{0,1:T(8,128)} dynamic-update-slice(f32[256,8192]{0,1:T(8,128)} %dynamic_update_slice.56, f32[16,8192]{0,1:T(8,128)} %copy.52, s32[]{:T(128)S(6)} %select_n.171, s32[]{:T(128)} %constant.156.clone.1) | dynamic-update-slice | bytes 1048580 | tf_op jit(solution)/shard_map/dynamic_update_slice | solution.py:26
  324.8 24.3 %dynamic_update_slice.58 = f32[256,8192]{0,1:T(8,128)} dynamic-update-slice(f32[256,8192]{0,1:T(8,128)} %dynamic_update_slice.57, f32[16,8192]{0,1:T(8,128)} %copy.53, s32[]{:T(128)S(6)} %select_n.173, s32[]{:T(128)} %constant.156.clone.1) | dynamic-update-slice | bytes 1048580 | tf_op jit(solution)/shard_map/dynamic_update_slice | solution.py:31
  351.8 23.4 %dynamic_update_slice.59 = f32[256,8192]{0,1:T(8,128)} dynamic-update-slice(f32[256,8192]{0,1:T(8,128)} %dynamic_update_slice.58, f32[16,8192]{0,1:T(8,128)} %copy.54, s32[]{:T(128)S(6)} %select_n.175, s32[]{:T(128)} %constant.156.clone.1) | dynamic-update-slice | bytes 1048580 | tf_op jit(solution)/shard_map/dynamic_update_slice | solution.py:26
  377.8 24.3 %dynamic_update_slice.60 = f32[256,8192]{0,1:T(8,128)} dynamic-update-slice(f32[256,8192]{0,1:T(8,128)} %dynamic_update_slice.59, f32[16,8192]{0,1:T(8,128)} %copy.55, s32[]{:T(128)S(6)} %select_n.177, s32[]{:T(128)} %constant.156.clone.1) | dynamic-update-slice | bytes 1048580 | tf_op jit(solution)/shard_map/dynamic_update_slice | solution.py:31
  431.5 24.3 %dynamic_update_slice.62 = f32[256,8192]{0,1:T(8,128)} dynamic-update-slice(f32[256,8192]{0,1:T(8,128)} %dynamic_update_slice.61, f32[16,8192]{0,1:T(8,128)} %copy.57, s32[]{:T(128)S(6)} %select_n.181, s32[]{:T(128)} %constant.156.clone.1) | dynamic-update-slice | bytes 1048580 | tf_op jit(solution)/shard_map/dynamic_update_slice | solution.py:31
  486.2 24.3 %dynamic_update_slice.64 = f32[256,8192]{0,1:T(8,128)} dynamic-update-slice(f32[256,8192]{0,1:T(8,128)} %dynamic_update_slice.63, f32[16,8192]{0,1:T(8,128)} %copy.59, s32[]{:T(128)S(6)} %select_n.185, s32[]{:T(128)} %constant.156.clone.1) | dynamic-update-slice | bytes 1048580 | tf_op jit(solution)/shard_map/dynamic_update_slice | solution.py:31
  539.9 24.3 %dynamic_update_slice.66 = f32[256,8192]{0,1:T(8,128)} dynamic-update-slice(f32[256,8192]{0,1:T(8,128)} %dynamic_update_slice.65, f32[16,8192]{0,1:T(8,128)} %copy.61, s32[]{:T(128)S(6)} %select_n.189, s32[]{:T(128)} %constant.156.clone.1) | dynamic-update-slice | bytes 1048580 | tf_op jit(solution)/shard_map/dynamic_update_slice | solution.py:31
  593.5 159.4 %while.43 = (s32[]{:T(128)}, f32[8,8,16,64,64]{3,4,2,1,0:T(8,128)}, s32[8]{0:T(128)S(1)}, pred[64,16]{1,0:T(8,128)(4,1)S(1)}, s32[64,16]{1,0:T(8,128)S(1)}, /*in...) while((s32[]{:T(128)}, f32[8,8,16,64,64]{3,4,2,1,0:T(8,128)}, ...), condition=%wide.region_3.4_spmd, body=%wide.region_2.3_spmd.sunk | while | flops 1611662720 | bytes 29892660 | solution.py:69
  776.8 23.5 %pmax.42 = f32[4096]{0:T(1024)S(1)} all-reduce(f32[4096]{0:T(1024)S(1)} %reshape.211), channel_id=1, replica_groups=mesh['item'=16,'code'=8] {'code'}, use_global_device_ids=true, to_apply=%region_7.8 | all-reduce | flops 4096 | bytes 32768 | tf_op jit(solution)/shard_map/pmax | solution.py:95
  800.3 24.7 %all-reduce.3 = (f32[4096]{0:T(1024)S(1)}, f32[]{:T(128)}) all-reduce(f32[4096]{0:T(1024)S(1)} %exponential_multiply_fusion.5, f32[]{:T(128)} %reduce_sum.73), channel_id=1, replica_groups=mesh['item'=16,'code'=8] {'code'}, use_global_device_ids=true, to_apply=%region_9.10 | all-reduce | flops 4097 | bytes 32776 | tf_op jit(solution)/shard_map/psum | solution.py:96
  878.5 69.5 %pmax.43 = f32[8192]{0:T(1024)S(1)} all-reduce(f32[8192]{0:T(1024)S(1)} %reshape.213), channel_id=1, replica_groups=mesh['item'=16,'code'=8] {'item'}, use_global_device_ids=true, to_apply=%region_14.15 | all-reduce | flops 8192 | bytes 65536 | tf_op jit(solution)/shard_map/pmax | solution.py:133
  948.0 69.7 %psum.59 = f32[8192]{0:T(1024)S(1)} all-reduce(f32[8192]{0:T(1024)S(1)} %exponential_multiply_fusion.2), channel_id=1, replica_groups=mesh['item'=16,'code'=8] {'item'}, use_global_device_ids=true, to_apply=%region_16.17 | all-reduce | flops 8192 | bytes 65536 | tf_op jit(solution)/shard_map/psum | solution.py:134
  1045.2 23.5 %pmax.44 = f32[4096]{0:T(1024)S(1)} all-reduce(f32[4096]{0:T(1024)S(1)} %reshape.219), channel_id=1, replica_groups=mesh['item'=16,'code'=8] {'code'}, use_global_device_ids=true, to_apply=%region_18.19 | all-reduce | flops 4096 | bytes 32768 | tf_op jit(solution)/shard_map/pmax | solution.py:95
  1068.8 23.6 %psum.60 = f32[4096]{0:T(1024)S(1)} all-reduce(f32[4096]{0:T(1024)S(1)} %exponential_multiply_fusion.4), channel_id=1, replica_groups=mesh['item'=16,'code'=8] {'code'}, use_global_device_ids=true, to_apply=%region_20.21 | all-reduce | flops 4096 | bytes 32768 | tf_op jit(solution)/shard_map/psum | solution.py:96
  1145.7 69.6 %pmax.45 = f32[8192]{0:T(1024)S(1)} all-reduce(f32[8192]{0:T(1024)S(1)} %reshape.221), channel_id=1, replica_groups=mesh['item'=16,'code'=8] {'item'}, use_global_device_ids=true, to_apply=%region_25.26 | all-reduce | flops 8192 | bytes 65536 | tf_op jit(solution)/shard_map/pmax | solution.py:133
  1215.3 69.5 %psum.61 = f32[8192]{0:T(1024)S(1)} all-reduce(f32[8192]{0:T(1024)S(1)} %exponential_multiply_fusion.1), channel_id=1, replica_groups=mesh['item'=16,'code'=8] {'item'}, use_global_device_ids=true, to_apply=%region_27.28 | all-reduce | flops 8192 | bytes 65536 | tf_op jit(solution)/shard_map/psum | solution.py:134
  1311.6 23.5 %pmax.46 = f32[4096]{0:T(1024)S(1)} all-reduce(f32[4096]{0:T(1024)S(1)} %reshape.226), channel_id=1, replica_groups=mesh['item'=16,'code'=8] {'code'}, use_global_device_ids=true, to_apply=%region_29.30 | all-reduce | flops 4096 | bytes 32768 | tf_op jit(solution)/shard_map/pmax | solution.py:95
  1335.2 23.8 %psum.62 = f32[4096]{0:T(1024)S(1)} all-reduce(f32[4096]{0:T(1024)S(1)} %exponential_multiply_fusion.3), channel_id=1, replica_groups=mesh['item'=16,'code'=8] {'code'}, use_global_device_ids=true, to_apply=%region_31.32 | all-reduce | flops 4096 | bytes 32768 | tf_op jit(solution)/shard_map/psum | solution.py:96
  1412.3 69.6 %pmax.47 = f32[8192]{0:T(1024)S(1)} all-reduce(f32[8192]{0:T(1024)S(1)} %reshape.228), channel_id=1, replica_groups=mesh['item'=16,'code'=8] {'item'}, use_global_device_ids=true, to_apply=%region_36.37 | all-reduce | flops 8192 | bytes 65536 | tf_op jit(solution)/shard_map/pmax | solution.py:133
  1481.9 69.5 %psum.63 = f32[8192]{0:T(1024)S(1)} all-reduce(f32[8192]{0:T(1024)S(1)} %exponential_multiply_fusion), channel_id=1, replica_groups=mesh['item'=16,'code'=8] {'item'}, use_global_device_ids=true, to_apply=%region_38.39 | all-reduce | flops 8192 | bytes 65536 | tf_op jit(solution)/shard_map/psum | solution.py:134
  (284 shorter events, 734.9 us)
Async XLA Ops:
  7.2 580.7 %all-gather.2.cloned.1.call-start = ((), (), s32[]{:S(2)}) async-start(), calls=%async_computation | async-start | bytes 4718592 | tf_op jit(solution)/shard_map/all_gather | solution.py:14
  7.9 18.8 %collective-permute-start = (f32[16,8192]{1,0:T(8,128)}, f32[16,8192]{1,0:T(8,128)S(1)}, u32[]{:S(2)}, u32[]{:S(2)}) collective-permute-start(f32[16,8192]{1,0:T(8,128)} %param.14), channel_id=1, source_target_pairs={{0,8},{8,16},{16,24},{24,32},{32,40},{40,48},{48,56},{56,64},{64,7... | collective-permute-start | bytes 1572872 | tf_op jit(solution)/shard_map/ppermute | solution.py:25
  9.6 17.1 %collective-permute-start.1 = (f32[16,8192]{1,0:T(8,128)}, f32[16,8192]{1,0:T(8,128)S(1)}, u32[]{:S(2)}, u32[]{:S(2)}) collective-permute-start(f32[16,8192]{1,0:T(8,128)} %param.14), channel_id=1, source_target_pairs={{0,120},{8,0},{16,8},{24,16},{32,24},{40,32},{48,40},{56,48},{64,5... | collective-permute-start | bytes 1572872 | tf_op jit(solution)/shard_map/ppermute | solution.py:30
  26.7 16.4 %collective-permute-start.2 = (f32[16,8192]{1,0:T(8,128)S(1)}, f32[16,8192]{1,0:T(8,128)S(1)}, u32[]{:S(2)}, u32[]{:S(2)}) collective-permute-start(f32[16,8192]{1,0:T(8,128)S(1)} %collective-permute-done), channel_id=1, source_target_pairs={{0,8},{8,16},{16,24},{24,32},{32,40},{40,48},{48,56},{56,64},{64,7... | collective-permute-start | bytes 1572872 | tf_op jit(solution)/shard_map/ppermute | solution.py:25
  26.7 16.4 %collective-permute-start.3 = (f32[16,8192]{1,0:T(8,128)S(1)}, f32[16,8192]{1,0:T(8,128)S(1)}, u32[]{:S(2)}, u32[]{:S(2)}) collective-permute-start(f32[16,8192]{1,0:T(8,128)S(1)} %collective-permute-done.1), channel_id=1, source_target_pairs={{0,120},{8,0},{16,8},{24,16},{32,24},{40,32},{48,40},{56,48},{64,5... | collective-permute-start | bytes 1572872 | tf_op jit(solution)/shard_map/ppermute | solution.py:30
  43.1 15.5 collective-permute-start.4
  43.1 15.5 collective-permute-start.5
  58.6 14.6 collective-permute-start.6
  59.4 13.8 collective-permute-start.7
  73.2 13.7 collective-permute-start.8
  74.0 87.7 %copy-start.12 = (f32[16,8192]{1,0:T(8,128)}, f32[16,8192]{1,0:T(8,128)S(1)}, u32[]{:S(2)}) copy-start(f32[16,8192]{1,0:T(8,128)S(1)} %collective-permute-done.7) | copy-start | bytes 1572868
  74.0 13.6 collective-permute-start.9
  86.9 12.8 collective-permute-start.10
  87.7 13.6 collective-permute-start.11
  99.7 13.2 collective-permute-start.12
  101.2 115.1 %copy-start.1 = (s32[1024]{0:T(1024)}, s32[1024]{0:T(1024)S(1)}, u32[]{:S(2)}) copy-start(s32[1024]{0:T(1024)S(1)} %broadcast_clamp_fusion.1) | copy-start | bytes 12292
  101.3 435.2 %collective-permute-start.13 = (f32[16,8192]{1,0:T(8,128)}, f32[16,8192]{1,0:T(8,128)}, u32[]{:S(2)}, u32[]{:S(2)}) collective-permute-start(f32[16,8192]{1,0:T(8,128)} %collective-permute-done.11), channel_id=1, source_target_pairs={{0,120},{8,0},{16,8},{24,16},{32,24},{40,32},{48,40},{56,48},{64,5... | collective-permute-start | bytes 1572872 | tf_op jit(solution)/shard_map/ppermute | solution.py:30
  112.9 451.3 %collective-permute-start.14 = (f32[16,8192]{1,0:T(8,128)S(1)}, f32[16,8192]{1,0:T(8,128)}, u32[]{:S(2)}, u32[]{:S(2)}) collective-permute-start(f32[16,8192]{1,0:T(8,128)S(1)} %collective-permute-done.12), channel_id=1, source_target_pairs={{0,8},{8,16},{16,24},{24,32},{32,40},{40,48},{48,56},{56,64},{64,7... | collective-permute-start | bytes 1572872 | tf_op jit(solution)/shard_map/ppermute | solution.py:25
  218.9 77.3 %copy-start.7 = (f32[16,8192]{1,0:T(8,128)S(1)}, f32[16,8192]{1,0:T(8,128)}, u32[]{:S(2)}) copy-start(f32[16,8192]{1,0:T(8,128)} %copy-done.6) | copy-start | bytes 1572868
  245.8 76.4 %copy-start.9 = (f32[16,8192]{1,0:T(8,128)S(1)}, f32[16,8192]{1,0:T(8,128)}, u32[]{:S(2)}) copy-start(f32[16,8192]{1,0:T(8,128)} %copy-done.8) | copy-start | bytes 1572868
  271.9 77.3 %copy-start.11 = (f32[16,8192]{1,0:T(8,128)S(1)}, f32[16,8192]{1,0:T(8,128)}, u32[]{:S(2)}) copy-start(f32[16,8192]{1,0:T(8,128)} %copy-done.10) | copy-start | bytes 1572868
  324.8 77.2 %copy-start.15 = (f32[16,8192]{1,0:T(8,128)S(1)}, f32[16,8192]{1,0:T(8,128)}, u32[]{:S(2)}) copy-start(f32[16,8192]{1,0:T(8,128)} %copy-done.14) | copy-start | bytes 1572868
  840.4 178.0 %copy-start.16 = (f32[8192]{0:T(1024)S(1)}, f32[8192]{0:T(1024)}, u32[]{:S(2)}) copy-start(f32[8192]{0:T(1024)} %param.16) | copy-start | bytes 98308
  840.4 178.1 %copy-start.2 = (s32[1024]{0:T(1024)S(1)}, s32[1024]{0:T(1024)}, u32[]{:S(2)}) copy-start(s32[1024]{0:T(1024)} %copy-done.1) | copy-start | bytes 12292
  (13 other events, 328.0 us)
Sparse Core Ops, SparseCore 0:
  9.7 34.5 all-gather.1
